TPU v7x, 128 devices: a whole 4x4x4 slice. The times are simulated.
128 devices in a mesh: section: 4 (over y), tensor: 32 (over z, x, core).
Axes of the slice: x: 4, y: 4, z: 4, core: 2. Of those that a mesh axis runs over, the one named last changes fastest.
Arguments:
- token_ids: int32 [4, 128], replicated, may hold values from 0 to 64127
- embedding: bfloat16 [64128, 8192], P('section', 'tensor'), may hold values from -6 to 6
- norm_gain: float32 [4, 8192], P('section'), may hold values from 0.1 to 1.9
- query_weight: bfloat16 [4, 8192, 8192], P('section', None, 'tensor'), may hold values from -0.0625 to 0.0625
- keyval_weight: bfloat16 [4, 8192, 2048], P('section', None, 'tensor'), may hold values from -0.0625 to 0.0625
- output_weight: bfloat16 [4, 8192, 8192], P('section', 'tensor'), may hold values from -0.0625 to 0.0625
- prefix_cache: bfloat16 [4, 128, 128, 2, 1024], P('section', 'tensor')
- prefix_lengths: int32 [128], P('tensor'), may hold values from 16 to 128, as said below
Outputs:
- answers: float32 [4, 128, 8192], P('section', 'tensor')
Inputs may be any that keep to these rules, and one draw needn't show every extreme that they name: `prefix_lengths`: some row has exactly 128 live positions.
All inputs are finite; a program needn't handle non-finite values.
Results may differ from a plain program's by a relative error of at most 0.039.
Values may be sent and summed in bfloat16 or wider, within the bound.
No kernel may reach another device: no remote copies, remote signals or barrier semaphores. Data moves between devices by JAX's collectives and lax.ppermute only.
A program may use at most 128 MiB of HBM per device.

v0:
```python
import jax
import jax.numpy as jnp
from jax import lax
from jax.sharding import PartitionSpec as P

HEADS = 64
KVH = 8
HD = 128
NORM_EPSILON = 1e-05
ROPE_BASE = 500000.0


def passed_along(block, axis, distance):
    devices = range(lax.axis_size(axis))
    route = [(i - distance, i) for i in devices if i - distance in devices]
    return lax.ppermute(block, axis, route)


def rope_tables(positions, head_dim):
    half_dim = head_dim // 2
    frequency = ROPE_BASE ** (-(jnp.arange(half_dim, dtype=jnp.float32) * 2.0 / head_dim))
    angles = positions.astype(jnp.float32)[:, None] * frequency[None, :]
    cosine = jnp.concatenate([jnp.cos(angles), jnp.cos(angles)], axis=-1)
    sine_table = jnp.concatenate([jnp.sin(angles), jnp.sin(angles)], axis=-1)
    return (cosine, sine_table)


def rotate(vectors, cosine, sine_table):
    half_dim = vectors.shape[-1] // 2
    swapped = jnp.concatenate([-vectors[..., half_dim:], vectors[..., :half_dim]], axis=-1)
    return vectors * cosine[:, None, :] + swapped * sine_table[:, None, :]


def normalize(values, gain_vec):
    scaling = lax.rsqrt(jnp.mean(values * values, axis=-1, keepdims=True) + NORM_EPSILON)
    return (values * scaling * gain_vec).astype(jnp.bfloat16)


def attend(queries, prefix, fresh_rows, live_len, step_index):
    row_count, kv_heads, group_size, head_dim = queries.shape
    step_total = fresh_rows.shape[0]
    past_keys = prefix[:, :, 0, :].reshape(row_count, -1, kv_heads, head_dim)
    past_vals = prefix[:, :, 1, :].reshape(row_count, -1, kv_heads, head_dim)
    new_keys = fresh_rows[:, :, 0, :].reshape(step_total, row_count, kv_heads, head_dim)
    new_vals = fresh_rows[:, :, 1, :].reshape(step_total, row_count, kv_heads, head_dim)
    score_scale = head_dim ** (-0.5)
    past_score = (
        jnp.einsum("rkgd,rlkd->rkgl", queries, past_keys, preferred_element_type=jnp.float32)
        * score_scale
    )
    new_score = (
        jnp.einsum("rkgd,srkd->rkgs", queries, new_keys, preferred_element_type=jnp.float32)
        * score_scale
    )
    past_mask = jnp.arange(past_keys.shape[1])[None, None, None, :] < live_len[:, None, None, None]
    new_mask = jnp.arange(step_total)[None, None, None, :] <= step_index
    past_score = jnp.where(past_mask, past_score, -1e30)
    new_score = jnp.where(new_mask, new_score, -1e30)
    top_score = jnp.maximum(jnp.max(past_score, axis=-1), jnp.max(new_score, axis=-1))[..., None]
    past_weight = jnp.exp(past_score - top_score)
    new_weight = jnp.exp(new_score - top_score)
    weight_total = jnp.sum(past_weight, axis=-1, keepdims=True) + jnp.sum(
        new_weight, axis=-1, keepdims=True
    )
    past_prob = (past_weight / weight_total).astype(jnp.bfloat16)
    new_prob = (new_weight / weight_total).astype(jnp.bfloat16)
    attended = jnp.einsum(
        "rkgl,rlkd->rkgd", past_prob, past_vals, preferred_element_type=jnp.float32
    )
    attended = attended + jnp.einsum(
        "rkgs,srkd->rkgd", new_prob, new_vals, preferred_element_type=jnp.float32
    )
    return attended.astype(jnp.bfloat16).reshape(row_count, kv_heads * group_size * head_dim)


def body(
    token_ids,
    embedding,
    norm_gain,
    query_weight,
    keyval_weight,
    output_weight,
    prefix_cache,
    prefix_lengths,
):
    n_tensor = lax.axis_size("tensor")
    section_pos = lax.axis_index("section")
    tensor_pos = lax.axis_index("tensor")
    last_section = lax.axis_size("section") - 1
    step_count = token_ids.shape[0]
    vocab_part = embedding.shape[0]
    own_rows = prefix_lengths.shape[0]
    model_width = embedding.shape[1] * n_tensor
    kv_width = KVH * HD
    group_size = HEADS // KVH
    local_ids = token_ids - section_pos * vocab_part
    inside = (local_ids >= 0) & (local_ids < vocab_part)
    picked = jnp.take(embedding, jnp.clip(local_ids, 0, vocab_part - 1), axis=0)
    partial_embed = jnp.where(inside[:, :, None], picked.astype(jnp.float32), 0.0)
    columns = lax.psum(partial_embed.astype(jnp.bfloat16), "section")
    own_embed = lax.all_to_all(columns, "tensor", split_axis=1, concat_axis=2, tiled=True)
    block_count = 1
    block_rows = own_rows // block_count
    item_count = step_count * block_count
    tick_count = item_count + last_section
    gain_vec = norm_gain[0]
    query_mat = query_weight[0]
    keyval_mat = keyval_weight[0]
    output_mat = output_weight[0]
    cache_rows = prefix_cache[0]
    carried = jnp.zeros((block_rows, model_width), jnp.float32)
    fresh_kv = jnp.zeros((step_count, own_rows, 2, kv_width), jnp.bfloat16)
    finals = jnp.zeros((step_count, own_rows, model_width), jnp.float32)

    def advance(tick_index, carry_state):
        incoming, fresh_kv, finals = carry_state
        item_index = tick_index - section_pos
        is_valid = (item_index >= 0) & (item_index < item_count)
        item_index = jnp.clip(item_index, 0, item_count - 1)
        step_index = item_index // block_count
        row_start = item_index % block_count * block_rows
        step_embed = lax.dynamic_index_in_dim(own_embed, step_index, 0, keepdims=False)
        first_input = step_embed.astype(jnp.float32)
        hidden_in = jnp.where(section_pos == 0, first_input, incoming)
        normed = lax.all_gather(normalize(hidden_in, gain_vec), "tensor", axis=0, tiled=True)
        queries = jnp.dot(normed, query_mat, preferred_element_type=jnp.float32)
        keyvals = jnp.dot(normed, keyval_mat, preferred_element_type=jnp.float32)
        queries, keyvals = (
            lax.all_to_all(queries, "tensor", split_axis=0, concat_axis=1, tiled=True),
            lax.all_to_all(keyvals, "tensor", split_axis=0, concat_axis=1, tiled=True),
        )
        cosine, sine_table = rope_tables(prefix_lengths + step_index, HD)
        turned_q = rotate(queries.reshape(block_rows, HEADS, HD), cosine, sine_table).astype(
            jnp.bfloat16
        )
        turned_k = rotate(
            keyvals[:, :kv_width].reshape(block_rows, KVH, HD), cosine, sine_table
        ).astype(jnp.bfloat16)
        value_cols = keyvals[:, kv_width:].astype(jnp.bfloat16)
        entry_kv = jnp.stack([turned_k.reshape(block_rows, kv_width), value_cols], axis=1)
        current = lax.dynamic_slice(
            fresh_kv, (step_index, row_start, 0, 0), (1, block_rows, 2, kv_width)
        )
        fresh_kv = lax.dynamic_update_slice(
            fresh_kv, jnp.where(is_valid, entry_kv[None], current), (step_index, row_start, 0, 0)
        )
        mixed_out = attend(
            turned_q.reshape(block_rows, KVH, group_size, HD),
            cache_rows,
            fresh_kv,
            prefix_lengths,
            step_index,
        )
        head_cols = lax.all_to_all(mixed_out, "tensor", split_axis=1, concat_axis=0, tiled=True)
        partial_value = (
            jnp.dot(head_cols, output_mat, preferred_element_type=jnp.float32)
            .astype(jnp.bfloat16)
            .astype(jnp.float32)
        )
        summed_all = lax.psum(partial_value.astype(jnp.bfloat16), "tensor").astype(jnp.float32)
        summed = lax.dynamic_slice_in_dim(summed_all, tensor_pos * block_rows, block_rows, 0)
        hidden_out = hidden_in + summed
        write_final = is_valid & (section_pos == last_section)
        current_final = lax.dynamic_slice(
            finals, (step_index, row_start, 0), (1, block_rows, model_width)
        )
        finals = lax.dynamic_update_slice(
            finals,
            jnp.where(write_final, hidden_out[None], current_final),
            (step_index, row_start, 0),
        )
        outgoing = passed_along(hidden_out, "section", 1)
        return (outgoing, fresh_kv, finals)

    spent, fresh_kv, finals = lax.fori_loop(0, tick_count, advance, (carried, fresh_kv, finals))
    answers = lax.psum_scatter(finals, "section", scatter_dimension=0, tiled=True)
    return answers


def solution(mesh):
    in_specs = (
        P(),
        P("section", "tensor"),
        P("section", None),
        P("section", None, "tensor"),
        P("section", None, "tensor"),
        P("section", "tensor", None),
        P("section", "tensor", None, None, None),
        P("tensor"),
    )
    out_specs = P("section", "tensor", None)
    return jax.shard_map(body, mesh=mesh, in_specs=in_specs, out_specs=out_specs, check_vma=False)
```

profile of v0, /device:TPU:0, one launch (start us, length us, event | category | flops | bytes accessed | tf_op | source)
XLA Modules:
  0.0 1589.0 jit_solution(3336385134684504714)
XLA Ops:
  15.2 44.3 %all-reduce.5.cloned.1.call-done = bf16[4,128,256]{2,0,1:T(4,128)(2,1)} async-done(((bf16[4,128,256]{2,0,1:T(4,128)(2,1)}), bf16[4,128,256]{2,0,1:T(4,128)(2,1)}) %all-reduce.5.cloned.1.call-update) | async-done | bytes 262160 | tf_op jit(solution)/shard_map/psum | solution.py:100
  76.9 1456.6 %while.19 = (s32[]{:T(128)}, f32[4,8192]{1,0:T(4,128)S(1)}, bf16[4,4,2,1024]{3,1,2,0:T(4,128)(2,1)S(1)}, f32[4,4,8192]{2,1,0:T(4,128)}, pred[]{:T(512)}, /*index...) while((s32[]{:T(128)}, f32[4,8192]{1,0:T(4,128)S(1)}, ...), condition=%wide.region_8.9_spmd, body=%wide.region_1.8_spmd.sunk | while | flops 1228397952 | bytes 74761704 | solution.py:175
  81.3 41.5 %all-gather.5.cloned.1.call-done = bf16[32,4,8192]{2,1,0:T(4,128)(2,1)} async-done(((bf16[1,4,8192]{2,1,0:T(4,128)(2,1)}), bf16[32,4,8192]{2,1,0:T(4,128)(2,1)}) %all-gather.5.cloned.1.call-update) | async-done | bytes 2097168 | tf_op jit(solution)/shard_map/while/body/eval_jaxpr/all_gather | solution.py:125
  155.0 11.0 all_to_all.139
  170.3 105.2 %all-reduce.9.cloned.1.call-done = bf16[128,8192]{1,0:T(8,128)(2,1)} async-done(((bf16[128,8192]{1,0:T(8,128)(2,1)}), bf16[128,8192]{1,0:T(8,128)(2,1)}) %all-reduce.9.cloned.1.call-update) | async-done | bytes 2097168 | tf_op jit(solution)/shard_map/while/body/eval_jaxpr/psum | solution.py:160
  287.8 43.3 %all-gather.5.cloned.1.call-done = bf16[32,4,8192]{2,1,0:T(4,128)(2,1)} async-done(((bf16[1,4,8192]{2,1,0:T(4,128)(2,1)}), bf16[32,4,8192]{2,1,0:T(4,128)(2,1)}) %all-gather.5.cloned.1.call-update) | async-done | bytes 2097168 | tf_op jit(solution)/shard_map/while/body/eval_jaxpr/all_gather | solution.py:125
  363.3 11.0 all_to_all.139
  378.6 105.2 %all-reduce.9.cloned.1.call-done = bf16[128,8192]{1,0:T(8,128)(2,1)} async-done(((bf16[128,8192]{1,0:T(8,128)(2,1)}), bf16[128,8192]{1,0:T(8,128)(2,1)}) %all-reduce.9.cloned.1.call-update) | async-done | bytes 2097168 | tf_op jit(solution)/shard_map/while/body/eval_jaxpr/psum | solution.py:160
  496.1 43.3 %all-gather.5.cloned.1.call-done = bf16[32,4,8192]{2,1,0:T(4,128)(2,1)} async-done(((bf16[1,4,8192]{2,1,0:T(4,128)(2,1)}), bf16[32,4,8192]{2,1,0:T(4,128)(2,1)}) %all-gather.5.cloned.1.call-update) | async-done | bytes 2097168 | tf_op jit(solution)/shard_map/while/body/eval_jaxpr/all_gather | solution.py:125
  571.6 11.0 all_to_all.139
  586.9 105.2 %all-reduce.9.cloned.1.call-done = bf16[128,8192]{1,0:T(8,128)(2,1)} async-done(((bf16[128,8192]{1,0:T(8,128)(2,1)}), bf16[128,8192]{1,0:T(8,128)(2,1)}) %all-reduce.9.cloned.1.call-update) | async-done | bytes 2097168 | tf_op jit(solution)/shard_map/while/body/eval_jaxpr/psum | solution.py:160
  704.4 43.7 %all-gather.5.cloned.1.call-done = bf16[32,4,8192]{2,1,0:T(4,128)(2,1)} async-done(((bf16[1,4,8192]{2,1,0:T(4,128)(2,1)}), bf16[32,4,8192]{2,1,0:T(4,128)(2,1)}) %all-gather.5.cloned.1.call-update) | async-done | bytes 2097168 | tf_op jit(solution)/shard_map/while/body/eval_jaxpr/all_gather | solution.py:125
  780.2 11.0 all_to_all.139
  795.5 105.2 %all-reduce.9.cloned.1.call-done = bf16[128,8192]{1,0:T(8,128)(2,1)} async-done(((bf16[128,8192]{1,0:T(8,128)(2,1)}), bf16[128,8192]{1,0:T(8,128)(2,1)}) %all-reduce.9.cloned.1.call-update) | async-done | bytes 2097168 | tf_op jit(solution)/shard_map/while/body/eval_jaxpr/psum | solution.py:160
  913.0 43.4 %all-gather.5.cloned.1.call-done = bf16[32,4,8192]{2,1,0:T(4,128)(2,1)} async-done(((bf16[1,4,8192]{2,1,0:T(4,128)(2,1)}), bf16[32,4,8192]{2,1,0:T(4,128)(2,1)}) %all-gather.5.cloned.1.call-update) | async-done | bytes 2097168 | tf_op jit(solution)/shard_map/while/body/eval_jaxpr/all_gather | solution.py:125
  988.5 11.0 all_to_all.139
  1003.8 105.2 %all-reduce.9.cloned.1.call-done = bf16[128,8192]{1,0:T(8,128)(2,1)} async-done(((bf16[128,8192]{1,0:T(8,128)(2,1)}), bf16[128,8192]{1,0:T(8,128)(2,1)}) %all-reduce.9.cloned.1.call-update) | async-done | bytes 2097168 | tf_op jit(solution)/shard_map/while/body/eval_jaxpr/psum | solution.py:160
  1121.3 43.3 %all-gather.5.cloned.1.call-done = bf16[32,4,8192]{2,1,0:T(4,128)(2,1)} async-done(((bf16[1,4,8192]{2,1,0:T(4,128)(2,1)}), bf16[32,4,8192]{2,1,0:T(4,128)(2,1)}) %all-gather.5.cloned.1.call-update) | async-done | bytes 2097168 | tf_op jit(solution)/shard_map/while/body/eval_jaxpr/all_gather | solution.py:125
  1196.8 11.0 all_to_all.139
  1212.1 105.2 %all-reduce.9.cloned.1.call-done = bf16[128,8192]{1,0:T(8,128)(2,1)} async-done(((bf16[128,8192]{1,0:T(8,128)(2,1)}), bf16[128,8192]{1,0:T(8,128)(2,1)}) %all-reduce.9.cloned.1.call-update) | async-done | bytes 2097168 | tf_op jit(solution)/shard_map/while/body/eval_jaxpr/psum | solution.py:160
  1329.6 43.3 %all-gather.5.cloned.1.call-done = bf16[32,4,8192]{2,1,0:T(4,128)(2,1)} async-done(((bf16[1,4,8192]{2,1,0:T(4,128)(2,1)}), bf16[32,4,8192]{2,1,0:T(4,128)(2,1)}) %all-gather.5.cloned.1.call-update) | async-done | bytes 2097168 | tf_op jit(solution)/shard_map/while/body/eval_jaxpr/all_gather | solution.py:125
  1405.1 11.0 all_to_all.139
  1420.4 105.3 %all-reduce.9.cloned.1.call-done = bf16[128,8192]{1,0:T(8,128)(2,1)} async-done(((bf16[128,8192]{1,0:T(8,128)(2,1)}), bf16[128,8192]{1,0:T(8,128)(2,1)}) %all-reduce.9.cloned.1.call-update) | async-done | bytes 2097168 | tf_op jit(solution)/shard_map/while/body/eval_jaxpr/psum | solution.py:160
  1535.3 44.9 %all-reduce.7.cloned.1.call-done = f32[4,4,8192]{2,1,0:T(4,128)} async-done(((f32[4,4,8192]{2,1,0:T(4,128)}), f32[4,4,8192]{2,1,0:T(4,128)}) %all-reduce.7.cloned.1.call-update) | async-done | bytes 524304
  (595 shorter events, 368.8 us)
Async XLA Ops:
  6.5 53.0 %all-reduce.5.cloned.1.call-start = ((), (), s32[]{:S(2)}) async-start(), calls=%async_computation.4 | async-start | bytes 524288 | tf_op jit(solution)/shard_map/psum | solution.py:100
  59.5 16.1 %all-to-all-start.3 = ((bf16[4,128,256]{2,0,1:T(4,128)(2,1)}), bf16[4,128,256]{2,0,1:T(4,128)(2,1)S(1)}, u32[]{:S(2)}, u32[]{:S(2)}) async-start(bf16[4,128,256]{2,0,1:T(4,128)(2,1)} %all-reduce.5.cloned.1.call-done), calls=%async_computation.3 | async-start | bytes 524288 | tf_op jit(solution)/shard_map/all_to_all | solution.py:101
  76.9 45.9 %all-gather.5.cloned.1.call-start = ((), (), s32[]{:S(2)}) async-start(), calls=%async_computation.6 | async-start | bytes 2162688 | tf_op jit(solution)/shard_map/while/body/eval_jaxpr/all_gather | solution.py:125
  128.3 12.6 all-to-all-start.1
  144.9 130.6 %all-reduce.9.cloned.1.call-start = ((), (), s32[]{:S(2)}) async-start(), calls=%async_computation.7 | async-start | bytes 4194304 | tf_op jit(solution)/shard_map/while/body/eval_jaxpr/psum | solution.py:160
  283.4 47.8 %all-gather.5.cloned.1.call-start = ((), (), s32[]{:S(2)}) async-start(), calls=%async_computation.6 | async-start | bytes 2162688 | tf_op jit(solution)/shard_map/while/body/eval_jaxpr/all_gather | solution.py:125
  336.7 12.6 all-to-all-start.1
  353.2 130.6 %all-reduce.9.cloned.1.call-start = ((), (), s32[]{:S(2)}) async-start(), calls=%async_computation.7 | async-start | bytes 4194304 | tf_op jit(solution)/shard_map/while/body/eval_jaxpr/psum | solution.py:160
  491.7 47.8 %all-gather.5.cloned.1.call-start = ((), (), s32[]{:S(2)}) async-start(), calls=%async_computation.6 | async-start | bytes 2162688 | tf_op jit(solution)/shard_map/while/body/eval_jaxpr/all_gather | solution.py:125
  545.0 12.6 all-to-all-start.1
  561.5 130.6 %all-reduce.9.cloned.1.call-start = ((), (), s32[]{:S(2)}) async-start(), calls=%async_computation.7 | async-start | bytes 4194304 | tf_op jit(solution)/shard_map/while/body/eval_jaxpr/psum | solution.py:160
  700.0 48.1 %all-gather.5.cloned.1.call-start = ((), (), s32[]{:S(2)}) async-start(), calls=%async_computation.6 | async-start | bytes 2162688 | tf_op jit(solution)/shard_map/while/body/eval_jaxpr/all_gather | solution.py:125
  753.6 12.6 all-to-all-start.1
  770.1 130.6 %all-reduce.9.cloned.1.call-start = ((), (), s32[]{:S(2)}) async-start(), calls=%async_computation.7 | async-start | bytes 4194304 | tf_op jit(solution)/shard_map/while/body/eval_jaxpr/psum | solution.py:160
  908.6 47.8 %all-gather.5.cloned.1.call-start = ((), (), s32[]{:S(2)}) async-start(), calls=%async_computation.6 | async-start | bytes 2162688 | tf_op jit(solution)/shard_map/while/body/eval_jaxpr/all_gather | solution.py:125
  961.9 12.6 all-to-all-start.1
  978.4 130.6 %all-reduce.9.cloned.1.call-start = ((), (), s32[]{:S(2)}) async-start(), calls=%async_computation.7 | async-start | bytes 4194304 | tf_op jit(solution)/shard_map/while/body/eval_jaxpr/psum | solution.py:160
  1116.9 47.8 %all-gather.5.cloned.1.call-start = ((), (), s32[]{:S(2)}) async-start(), calls=%async_computation.6 | async-start | bytes 2162688 | tf_op jit(solution)/shard_map/while/body/eval_jaxpr/all_gather | solution.py:125
  1170.2 12.6 all-to-all-start.1
  1186.7 130.6 %all-reduce.9.cloned.1.call-start = ((), (), s32[]{:S(2)}) async-start(), calls=%async_computation.7 | async-start | bytes 4194304 | tf_op jit(solution)/shard_map/while/body/eval_jaxpr/psum | solution.py:160
  1325.2 47.8 %all-gather.5.cloned.1.call-start = ((), (), s32[]{:S(2)}) async-start(), calls=%async_computation.6 | async-start | bytes 2162688 | tf_op jit(solution)/shard_map/while/body/eval_jaxpr/all_gather | solution.py:125
  1378.5 12.6 all-to-all-start.1
  1395.0 130.6 %all-reduce.9.cloned.1.call-start = ((), (), s32[]{:S(2)}) async-start(), calls=%async_computation.7 | async-start | bytes 4194304 | tf_op jit(solution)/shard_map/while/body/eval_jaxpr/psum | solution.py:160
  1533.5 46.7 %all-reduce.7.cloned.1.call-start = ((), (), s32[]{:S(2)}) async-start(), calls=%async_computation.5 | async-start | bytes 1048576
  (94 other events, 3158.5 us)
Sparse Core Ops, SparseCore 0:
  15.4 44.1 all-reduce.4
  80.3 42.4 all-gather.4
  170.4 105.0 all-reduce.8
  286.4 44.6 all-gather.4
  378.7 105.0 all-reduce.8
  494.7 44.6 all-gather.4
  587.0 105.0 all-reduce.8
  703.3 44.6 all-gather.4
  795.6 105.0 all-reduce.8
  911.6 44.6 all-gather.4
  1003.9 105.0 all-reduce.8
  1119.9 44.6 all-gather.4
  1212.2 105.0 all-reduce.8
  1328.2 44.6 all-gather.4
  1420.5 105.0 all-reduce.8
  1536.5 43.7 all-reduce.6
where the time goes:
time: 1590 us
  waiting for transfers between devices  1210 us (76%)
  starting transfers between devices  95.2 us (6%)
  matrix products  77.1 us (5%)
  blocking collectives  76.7 us (5%)
  local copies, waits for them, and re-layouts  60.2 us (4%)
  other arithmetic  50.7 us (3%)
    psum x7, waiting for transfers between devices, advance(): lax.psum(partial_value.astype(jnp.bfloat16), 'tensor').astype(jnp.float32)  737 us
    all_gather x7, waiting for transfers between devices, advance(): lax.all_gather(normalize(hidden_in, gain_vec), 'tensor', axis=0, tiled=True)  302 us
    all_to_all x7, blocking collectives, advance(): lax.all_to_all(mixed_out, 'tensor', split_axis=1, concat_axis=0, tiled=True)  76.7 us
    unnamed x3, waiting for transfers between devices  45.4 us
    psum x1, waiting for transfers between devices, body(): columns = lax.psum(partial_embed.astype(jnp.bfloat16), 'section')  44.3 us
    all_to_all x7, waiting for transfers between devices, advance(): lax.all_to_all(queries, 'tensor', split_axis=0, concat_axis=1, tiled=True)  37.2 us
    all_to_all x7, starting transfers between devices, advance(): lax.all_to_all(keyvals, 'tensor', split_axis=0, concat_axis=1, tiled=True)  36.6 us
  transfers between devices with their start and end apart: 38, of which 38 were waited for; matrix products, arithmetic and copies ran while one was open for 4% of the time, Pallas kernels for 0%

commit v1 on v0

--- a/solution.py
+++ b/solution.py
@@ -127,7 +127,12 @@
         keyvals = jnp.dot(normed, keyval_mat, preferred_element_type=jnp.float32)
         queries, keyvals = (
             lax.all_to_all(queries, "tensor", split_axis=0, concat_axis=1, tiled=True),
-            lax.all_to_all(keyvals, "tensor", split_axis=0, concat_axis=1, tiled=True),
+            jnp.concatenate(
+                lax.all_to_all(
+                    jnp.stack(jnp.split(keyvals, lax.axis_size("tensor"), axis=0)), "tensor", 0, 0
+                ),
+                axis=1,
+            ),
         )
         cosine, sine_table = rope_tables(prefix_lengths + step_index, HD)
         turned_q = rotate(queries.reshape(block_rows, HEADS, HD), cosine, sine_table).astype(

time: 1590 us -> 1760 us (1.11)
  local copies, waits for them, and re-layouts: 60.2 us -> 223 us
    while x196 -> x413, local copies, waits for them, and re-layouts: 23.7 us -> 170 us
where the time goes in v1:
time: 1760 us; the launch traced here: 1750 us
  waiting for transfers between devices  1210 us (69%)
  local copies, waits for them, and re-layouts  223 us (13%)
  starting transfers between devices  95.2 us (5%)
  matrix products  79.4 us (5%)
  blocking collectives  76.7 us (4%)
  other arithmetic  50.7 us (3%)
    psum x7, waiting for transfers between devices, advance(): lax.psum(partial_value.astype(jnp.bfloat16), 'tensor').astype(jnp.float32)  737 us
    all_gather x7, waiting for transfers between devices, advance(): lax.all_gather(normalize(hidden_in, gain_vec), 'tensor', axis=0, tiled=True)  302 us
    while x413, local copies, waits for them, and re-layouts  170 us
    all_to_all x7, blocking collectives, advance(): lax.all_to_all(mixed_out, 'tensor', split_axis=1, concat_axis=0, tiled=True)  76.7 us
    unnamed x3, waiting for transfers between devices  45.4 us
    psum x1, waiting for transfers between devices, body(): columns = lax.psum(partial_embed.astype(jnp.bfloat16), 'section')  44.3 us
    all_to_all x7, waiting for transfers between devices, advance(): lax.all_to_all(queries, 'tensor', split_axis=0, concat_axis=1, tiled=True)  37.2 us
    all_to_all x7, starting transfers between devices, advance(): lax.all_to_all(jnp.stack(jnp.split(keyvals, lax.axis_size('tensor'), axis...  36.6 us
  transfers between devices with their start and end apart: 38, of which 38 were waited for; matrix products, arithmetic and copies ran while one was open for 4% of the time, Pallas kernels for 0%

profile of v1, /device:TPU:0, one launch (start us, length us, event | category | flops | bytes accessed | tf_op | source)
XLA Modules:
  0.0 1754.1 jit_solution(12470725899415868860)
XLA Ops:
  15.2 44.3 %all-reduce.5.cloned.1.call-done = bf16[4,128,256]{2,0,1:T(4,128)(2,1)} async-done(((bf16[4,128,256]{2,0,1:T(4,128)(2,1)}), bf16[4,128,256]{2,0,1:T(4,128)(2,1)}) %all-reduce.5.cloned.1.call-update) | async-done | bytes 262160 | tf_op jit(solution)/shard_map/psum | solution.py:100
  76.9 1621.7 %while.19 = (s32[]{:T(128)}, f32[4,8192]{1,0:T(4,128)S(1)}, bf16[4,4,2,1024]{3,1,2,0:T(4,128)(2,1)S(1)}, f32[4,4,8192]{2,1,0:T(4,128)}, pred[]{:T(512)}, /*index...) while((s32[]{:T(128)}, f32[4,8192]{1,0:T(4,128)S(1)}, ...), condition=%wide.region_8.9_spmd, body=%wide.region_1.8_spmd.sunk | while | flops 1228397952 | bytes 75908584 | solution.py:180
  81.3 41.5 %all-gather.5.cloned.1.call-done = bf16[32,4,8192]{2,1,0:T(4,128)(2,1)} async-done(((bf16[1,4,8192]{2,1,0:T(4,128)(2,1)}), bf16[32,4,8192]{2,1,0:T(4,128)(2,1)}) %all-gather.5.cloned.1.call-update) | async-done | bytes 2097168 | tf_op jit(solution)/shard_map/while/body/eval_jaxpr/all_gather | solution.py:125
  178.6 11.0 all_to_all.110
  193.8 105.2 %all-reduce.9.cloned.1.call-done = bf16[128,8192]{1,0:T(8,128)(2,1)} async-done(((bf16[128,8192]{1,0:T(8,128)(2,1)}), bf16[128,8192]{1,0:T(8,128)(2,1)}) %all-reduce.9.cloned.1.call-update) | async-done | bytes 2097168 | tf_op jit(solution)/shard_map/while/body/eval_jaxpr/psum | solution.py:165
  311.3 43.3 %all-gather.5.cloned.1.call-done = bf16[32,4,8192]{2,1,0:T(4,128)(2,1)} async-done(((bf16[1,4,8192]{2,1,0:T(4,128)(2,1)}), bf16[32,4,8192]{2,1,0:T(4,128)(2,1)}) %all-gather.5.cloned.1.call-update) | async-done | bytes 2097168 | tf_op jit(solution)/shard_map/while/body/eval_jaxpr/all_gather | solution.py:125
  410.5 11.0 all_to_all.110
  425.7 105.2 %all-reduce.9.cloned.1.call-done = bf16[128,8192]{1,0:T(8,128)(2,1)} async-done(((bf16[128,8192]{1,0:T(8,128)(2,1)}), bf16[128,8192]{1,0:T(8,128)(2,1)}) %all-reduce.9.cloned.1.call-update) | async-done | bytes 2097168 | tf_op jit(solution)/shard_map/while/body/eval_jaxpr/psum | solution.py:165
  543.2 43.3 %all-gather.5.cloned.1.call-done = bf16[32,4,8192]{2,1,0:T(4,128)(2,1)} async-done(((bf16[1,4,8192]{2,1,0:T(4,128)(2,1)}), bf16[32,4,8192]{2,1,0:T(4,128)(2,1)}) %all-gather.5.cloned.1.call-update) | async-done | bytes 2097168 | tf_op jit(solution)/shard_map/while/body/eval_jaxpr/all_gather | solution.py:125
  642.4 11.0 all_to_all.110
  657.6 105.2 %all-reduce.9.cloned.1.call-done = bf16[128,8192]{1,0:T(8,128)(2,1)} async-done(((bf16[128,8192]{1,0:T(8,128)(2,1)}), bf16[128,8192]{1,0:T(8,128)(2,1)}) %all-reduce.9.cloned.1.call-update) | async-done | bytes 2097168 | tf_op jit(solution)/shard_map/while/body/eval_jaxpr/psum | solution.py:165
  775.1 43.7 %all-gather.5.cloned.1.call-done = bf16[32,4,8192]{2,1,0:T(4,128)(2,1)} async-done(((bf16[1,4,8192]{2,1,0:T(4,128)(2,1)}), bf16[32,4,8192]{2,1,0:T(4,128)(2,1)}) %all-gather.5.cloned.1.call-update) | async-done | bytes 2097168 | tf_op jit(solution)/shard_map/while/body/eval_jaxpr/all_gather | solution.py:125
  874.6 11.0 all_to_all.110
  889.8 105.2 %all-reduce.9.cloned.1.call-done = bf16[128,8192]{1,0:T(8,128)(2,1)} async-done(((bf16[128,8192]{1,0:T(8,128)(2,1)}), bf16[128,8192]{1,0:T(8,128)(2,1)}) %all-reduce.9.cloned.1.call-update) | async-done | bytes 2097168 | tf_op jit(solution)/shard_map/while/body/eval_jaxpr/psum | solution.py:165
  1007.3 43.4 %all-gather.5.cloned.1.call-done = bf16[32,4,8192]{2,1,0:T(4,128)(2,1)} async-done(((bf16[1,4,8192]{2,1,0:T(4,128)(2,1)}), bf16[32,4,8192]{2,1,0:T(4,128)(2,1)}) %all-gather.5.cloned.1.call-update) | async-done | bytes 2097168 | tf_op jit(solution)/shard_map/while/body/eval_jaxpr/all_gather | solution.py:125
  1106.5 11.0 all_to_all.110
  1121.7 105.2 %all-reduce.9.cloned.1.call-done = bf16[128,8192]{1,0:T(8,128)(2,1)} async-done(((bf16[128,8192]{1,0:T(8,128)(2,1)}), bf16[128,8192]{1,0:T(8,128)(2,1)}) %all-reduce.9.cloned.1.call-update) | async-done | bytes 2097168 | tf_op jit(solution)/shard_map/while/body/eval_jaxpr/psum | solution.py:165
  1239.2 43.3 %all-gather.5.cloned.1.call-done = bf16[32,4,8192]{2,1,0:T(4,128)(2,1)} async-done(((bf16[1,4,8192]{2,1,0:T(4,128)(2,1)}), bf16[32,4,8192]{2,1,0:T(4,128)(2,1)}) %all-gather.5.cloned.1.call-update) | async-done | bytes 2097168 | tf_op jit(solution)/shard_map/while/body/eval_jaxpr/all_gather | solution.py:125
  1338.3 11.0 all_to_all.110
  1353.6 105.2 %all-reduce.9.cloned.1.call-done = bf16[128,8192]{1,0:T(8,128)(2,1)} async-done(((bf16[128,8192]{1,0:T(8,128)(2,1)}), bf16[128,8192]{1,0:T(8,128)(2,1)}) %all-reduce.9.cloned.1.call-update) | async-done | bytes 2097168 | tf_op jit(solution)/shard_map/while/body/eval_jaxpr/psum | solution.py:165
  1471.1 43.3 %all-gather.5.cloned.1.call-done = bf16[32,4,8192]{2,1,0:T(4,128)(2,1)} async-done(((bf16[1,4,8192]{2,1,0:T(4,128)(2,1)}), bf16[32,4,8192]{2,1,0:T(4,128)(2,1)}) %all-gather.5.cloned.1.call-update) | async-done | bytes 2097168 | tf_op jit(solution)/shard_map/while/body/eval_jaxpr/all_gather | solution.py:125
  1570.2 11.0 all_to_all.110
  1585.5 105.2 %all-reduce.9.cloned.1.call-done = bf16[128,8192]{1,0:T(8,128)(2,1)} async-done(((bf16[128,8192]{1,0:T(8,128)(2,1)}), bf16[128,8192]{1,0:T(8,128)(2,1)}) %all-reduce.9.cloned.1.call-update) | async-done | bytes 2097168 | tf_op jit(solution)/shard_map/while/body/eval_jaxpr/psum | solution.py:165
  1700.4 44.9 %all-reduce.7.cloned.1.call-done = f32[4,4,8192]{2,1,0:T(4,128)} async-done(((f32[4,4,8192]{2,1,0:T(4,128)}), f32[4,4,8192]{2,1,0:T(4,128)}) %all-reduce.7.cloned.1.call-update) | async-done | bytes 524304
  (826 shorter events, 533.7 us)
Async XLA Ops:
  6.5 53.0 %all-reduce.5.cloned.1.call-start = ((), (), s32[]{:S(2)}) async-start(), calls=%async_computation.4 | async-start | bytes 524288 | tf_op jit(solution)/shard_map/psum | solution.py:100
  59.5 16.1 all-to-all-start.3
  76.9 45.9 %all-gather.5.cloned.1.call-start = ((), (), s32[]{:S(2)}) async-start(), calls=%async_computation.6 | async-start | bytes 2162688 | tf_op jit(solution)/shard_map/while/body/eval_jaxpr/all_gather | solution.py:125
  151.9 12.6 all-to-all-start.1
  168.4 130.6 %all-reduce.9.cloned.1.call-start = ((), (), s32[]{:S(2)}) async-start(), calls=%async_computation.7 | async-start | bytes 4194304 | tf_op jit(solution)/shard_map/while/body/eval_jaxpr/psum | solution.py:165
  306.9 47.8 %all-gather.5.cloned.1.call-start = ((), (), s32[]{:S(2)}) async-start(), calls=%async_computation.6 | async-start | bytes 2162688 | tf_op jit(solution)/shard_map/while/body/eval_jaxpr/all_gather | solution.py:125
  383.8 12.6 all-to-all-start.1
  400.3 130.6 %all-reduce.9.cloned.1.call-start = ((), (), s32[]{:S(2)}) async-start(), calls=%async_computation.7 | async-start | bytes 4194304 | tf_op jit(solution)/shard_map/while/body/eval_jaxpr/psum | solution.py:165
  538.8 47.8 %all-gather.5.cloned.1.call-start = ((), (), s32[]{:S(2)}) async-start(), calls=%async_computation.6 | async-start | bytes 2162688 | tf_op jit(solution)/shard_map/while/body/eval_jaxpr/all_gather | solution.py:125
  615.7 12.6 all-to-all-start.1
  632.2 130.6 %all-reduce.9.cloned.1.call-start = ((), (), s32[]{:S(2)}) async-start(), calls=%async_computation.7 | async-start | bytes 4194304 | tf_op jit(solution)/shard_map/while/body/eval_jaxpr/psum | solution.py:165
  770.7 48.1 %all-gather.5.cloned.1.call-start = ((), (), s32[]{:S(2)}) async-start(), calls=%async_computation.6 | async-start | bytes 2162688 | tf_op jit(solution)/shard_map/while/body/eval_jaxpr/all_gather | solution.py:125
  847.9 12.6 all-to-all-start.1
  864.4 130.6 %all-reduce.9.cloned.1.call-start = ((), (), s32[]{:S(2)}) async-start(), calls=%async_computation.7 | async-start | bytes 4194304 | tf_op jit(solution)/shard_map/while/body/eval_jaxpr/psum | solution.py:165
  1002.9 47.8 %all-gather.5.cloned.1.call-start = ((), (), s32[]{:S(2)}) async-start(), calls=%async_computation.6 | async-start | bytes 2162688 | tf_op jit(solution)/shard_map/while/body/eval_jaxpr/all_gather | solution.py:125
  1079.8 12.6 all-to-all-start.1
  1096.3 130.6 %all-reduce.9.cloned.1.call-start = ((), (), s32[]{:S(2)}) async-start(), calls=%async_computation.7 | async-start | bytes 4194304 | tf_op jit(solution)/shard_map/while/body/eval_jaxpr/psum | solution.py:165
  1234.8 47.8 %all-gather.5.cloned.1.call-start = ((), (), s32[]{:S(2)}) async-start(), calls=%async_computation.6 | async-start | bytes 2162688 | tf_op jit(solution)/shard_map/while/body/eval_jaxpr/all_gather | solution.py:125
  1311.7 12.6 all-to-all-start.1
  1328.2 130.6 %all-reduce.9.cloned.1.call-start = ((), (), s32[]{:S(2)}) async-start(), calls=%async_computation.7 | async-start | bytes 4194304 | tf_op jit(solution)/shard_map/while/body/eval_jaxpr/psum | solution.py:165
  1466.7 47.8 %all-gather.5.cloned.1.call-start = ((), (), s32[]{:S(2)}) async-start(), calls=%async_computation.6 | async-start | bytes 2162688 | tf_op jit(solution)/shard_map/while/body/eval_jaxpr/all_gather | solution.py:125
  1543.6 12.6 all-to-all-start.1
  1560.1 130.6 %all-reduce.9.cloned.1.call-start = ((), (), s32[]{:S(2)}) async-start(), calls=%async_computation.7 | async-start | bytes 4194304 | tf_op jit(solution)/shard_map/while/body/eval_jaxpr/psum | solution.py:165
  1698.6 46.7 %all-reduce.7.cloned.1.call-start = ((), (), s32[]{:S(2)}) async-start(), calls=%async_computation.5 | async-start | bytes 1048576
  (94 other events, 3158.5 us)
Sparse Core Ops, SparseCore 0:
  15.4 44.1 all-reduce.4
  80.3 42.4 all-gather.4
  194.0 105.0 all-reduce.8
  310.0 44.6 all-gather.4
  425.9 105.0 all-reduce.8
  541.9 44.6 all-gather.4
  657.7 105.0 all-reduce.8
  774.1 44.6 all-gather.4
  890.0 105.0 all-reduce.8
  1006.0 44.6 all-gather.4
  1121.8 105.0 all-reduce.8
  1237.9 44.6 all-gather.4
  1353.7 105.0 all-reduce.8
  1469.7 44.6 all-gather.4
  1585.6 105.0 all-reduce.8
  1701.6 43.7 all-reduce.6
